TPU v7x, 256 devices: a whole 4x4x8 slice. The times are simulated.
256 devices in a mesh: dp: 8 (over y, core), label: 32 (over x, z).
Axes of the slice: x: 4, y: 4, z: 8, core: 2. Of those that a mesh axis runs over, the one named last changes fastest.
Arguments:
- encoded: bfloat16 [32768, 1024], P(('dp', 'label')), may hold values from -6 to 6
- positive_clusters: int32 [32768, 4], P(('dp', 'label')), may hold values from 0 to 16383
- cluster_weight: bfloat16 [16384, 1024], P('label'), may hold values from -0.1875 to 0.1875
- shortlist: int32 [32768, 4], P(('dp', 'label')), may hold values from 0 to 511, all different within a row; in each aligned block of 128 rows (0 to 127, 128 to 255, ...) at most 2 rows name the same one
- positive_offsets: int32 [32768, 4], P(('dp', 'label')), may hold values from 0 to 127
- block_weight: bfloat16 [512, 128, 1024], P('label'), may hold values from -0.1875 to 0.1875
Outputs:
- grad_hidden: bfloat16 [32768, 1024], P(('dp', 'label'))
- grad_cluster: float32 [16384, 1024], P('label', 'dp')
- grad_block: float32 [512, 128, 1024], P('label', None, 'dp')
Inputs may be any that keep to these rules, and one draw needn't show every extreme that they name: `shortlist`: each row names 4 different blocks. Among the rows of one device no block is named more than 2 times, and in every draw some block is named exactly 2 times by the rows of some device.
All inputs are finite; a program needn't handle non-finite values.
Results may differ from a plain program's by a relative error of at most 0.018.
Values may be sent and summed in bfloat16 or wider, within the bound.
A program may use at most 128 MiB of HBM per device.

v0:
```python
import math
import jax
import jax.numpy as jnp
from jax import lax
from jax.sharding import PartitionSpec as P


def per_device(
    encoded, positive_clusters, cluster_weight, shortlist, positive_offsets, block_weight
):
    doc_rows, width = encoded.shape
    label_count = lax.axis_size("label")
    label_index = lax.axis_index("label")
    clusters_dev = cluster_weight.shape[0]
    rows_all = doc_rows * label_count
    scale = 1.0 / math.sqrt(rows_all * lax.axis_size("dp"))
    cluster_ids = label_index * clusters_dev + jnp.arange(clusters_dev, dtype=jnp.int32)
    rows = lax.all_gather(encoded, "label", axis=0, tiled=True)
    positives = lax.all_gather(positive_clusters, "label", axis=0, tiled=True)
    scores = lax.dot_general(
        rows, cluster_weight, (((1,), (1,)), ((), ())), preferred_element_type=jnp.float32
    )
    hits = jnp.any(positives[:, :, None] == cluster_ids[None, None, :], axis=1)
    delta = (jax.nn.sigmoid(scores) - hits.astype(jnp.float32)).astype(jnp.bfloat16)
    grad_sum = lax.dot_general(
        delta, rows, (((0,), (0,)), ((), ())), preferred_element_type=jnp.float32
    )
    deltas = delta
    grad_cluster, deltas = (grad_sum, deltas)
    products = jnp.dot(deltas, cluster_weight, preferred_element_type=jnp.float32)
    hidden_one = lax.psum_scatter(
        products.astype(jnp.bfloat16), "label", scatter_dimension=0, tiled=True
    ).astype(jnp.float32)
    listed = shortlist.shape[1]
    pairs = doc_rows * listed
    blocks_dev, block_len, _ = block_weight.shape
    blocks_total = blocks_dev * label_count
    capacity = max(2, 2 * pairs // blocks_total)
    slots_total = blocks_total * capacity
    flat_block = shortlist.reshape(-1)
    onehot = (flat_block[:, None] == jnp.arange(blocks_total, dtype=jnp.int32)[None, :]).astype(
        jnp.bfloat16
    )
    lower = (jnp.arange(pairs)[:, None] > jnp.arange(pairs)[None, :]).astype(jnp.bfloat16)
    earlier = jnp.dot(lower, onehot, preferred_element_type=jnp.float32)
    rank = jnp.sum(earlier * onehot.astype(jnp.float32), axis=1).astype(jnp.int32)
    slot = flat_block * capacity + rank
    source = (
        jnp.full((slots_total,), -1, jnp.int32).at[slot].set(jnp.arange(pairs, dtype=jnp.int32))
    )
    filled = source >= 0
    picked = jnp.maximum(source, 0)
    send_rows = jnp.where(filled[:, None], encoded[picked // listed], jnp.zeros((), jnp.bfloat16))
    send_offsets = jnp.where(filled, positive_offsets.reshape(-1)[picked], -1)
    send_rows = send_rows.reshape(label_count, blocks_dev * capacity, width)
    send_offsets = send_offsets.reshape(label_count, blocks_dev * capacity)
    got_rows, got_offsets = (
        lax.all_to_all(send_rows, "label", split_axis=0, concat_axis=0, tiled=True),
        lax.all_to_all(send_offsets, "label", split_axis=0, concat_axis=0, tiled=True),
    )
    arrived = got_rows.reshape(label_count, blocks_dev, capacity, width)
    offsets = got_offsets.reshape(label_count, blocks_dev, capacity)
    scores = jnp.einsum("sbcd,bld->sbcl", arrived, block_weight, preferred_element_type=jnp.float32)
    target = (offsets[..., None] == jnp.arange(block_len, dtype=jnp.int32)).astype(jnp.float32)
    delta = jnp.where((offsets >= 0)[..., None], jax.nn.sigmoid(scores) - target, 0.0).astype(
        jnp.bfloat16
    )
    back = jnp.einsum(
        "sbcl,bld->sbcd", delta, block_weight, preferred_element_type=jnp.float32
    ).astype(jnp.bfloat16)
    grad_block = jnp.einsum("sbcl,sbcd->bld", delta, arrived, preferred_element_type=jnp.float32)
    returned = lax.all_to_all(
        back.reshape(label_count, blocks_dev * capacity, width),
        "label",
        split_axis=0,
        concat_axis=0,
        tiled=True,
    )
    per_pair = returned.reshape(slots_total, width)[slot].astype(jnp.float32)
    hidden_two = jnp.sum(per_pair.reshape(doc_rows, listed, width), axis=1)
    grad_hidden = (hidden_one + hidden_two).astype(jnp.bfloat16)
    cluster_share, block_share = (
        lax.psum_scatter(
            (grad_cluster * scale).astype(jnp.bfloat16), "dp", scatter_dimension=1, tiled=True
        ).astype(jnp.float32),
        lax.psum_scatter(
            (grad_block * scale).reshape(blocks_dev * block_len, width).astype(jnp.bfloat16),
            "dp",
            scatter_dimension=1,
            tiled=True,
        ).astype(jnp.float32),
    )
    return (grad_hidden, cluster_share, block_share.reshape(blocks_dev, block_len, -1))


def solution(mesh):
    placed = (
        P(("dp", "label"), None),
        P(("dp", "label"), None),
        P("label", None),
        P(("dp", "label"), None),
        P(("dp", "label"), None),
        P("label", None, None),
    )
    return jax.shard_map(
        per_device,
        mesh=mesh,
        in_specs=placed,
        out_specs=(P(("dp", "label"), None), P("label", "dp"), P("label", None, "dp")),
        check_vma=False,
    )
```

profile of v0, /device:TPU:8, one launch (start us, length us, event | category | flops | bytes accessed | tf_op | source)
XLA Modules:
  0.0 472.1 jit_solution(16597565565228183674)
XLA Ops:
  12.0 2.4 scatter_custom_fusion
  14.5 6.9 %gather_fusion = s32[1024]{0:T(1024)S(1)} fusion(s32[512]{0:T(512)S(1)} %reshape.92, s32[1024]{0:T(1024)S(1)} %maximum_clamp_fusion), kind=kCustom, calls=%fused_computation | custom fusion | bytes 12288 | tf_op jit(solution)/shard_map/gather | solution.py:54
  22.1 11.3 %all-to-all-start = ((s32[32,1,32]{2,1,0:T(1,128)}), s32[32,1,32]{2,1,0:T(1,128)S(1)}, u32[]{:S(2)}, u32[]{:S(2)}) async-start(s32[32,1,32]{2,1,0:T(1,128)} %bitcast.2), calls=%async_computation.1 | async-start | bytes 32768 | tf_op jit(solution)/shard_map/all_to_all | solution.py:59
  33.5 4.1 gather_fusion.1
  39.1 4.1 all-to-all-done
  43.2 5.7 %all-to-all-start.1 = ((bf16[32,32,1024]{2,1,0:T(8,128)(2,1)}), bf16[32,32,1024]{2,1,0:T(8,128)(2,1)S(1)}, u32[]{:S(2)}, u32[]{:S(2)}) async-start(bf16[32,32,1024]{2,1,0:T(8,128)(2,1)} %broadcast_select_fusion), calls=%async_computation.2 | async-start | bytes 4194304 | tf_op jit(solution)/shard_map/all_to_all | solution.py:58
  49.1 64.0 %all-to-all-done.1 = bf16[32,32,1024]{2,1,0:T(8,128)(2,1)S(1)} async-done(((bf16[32,32,1024]{2,1,0:T(8,128)(2,1)}), bf16[32,32,1024]{2,1,0:T(8,128)(2,1)S(1)}, u32[]{:S(2)}, u32[]{:S(2)}) %all-to-all-start.1) | async-done | bytes 2097184 | tf_op jit(solution)/shard_map/all_to_all | solution.py:58
  115.4 1.7 fusion.30
  117.1 3.2 fusion
  120.4 6.5 %copy.48 = bf16[2048,1024]{0,1:T(8,128)(2,1)} copy(bf16[2048,1024]{1,0:T(8,128)(2,1)} %bitcast.68) | data formatting | bytes 8388608
  127.5 48.2 %all_gather.7 = s32[4096,4]{0,1:T(4,128)S(1)} all-gather(s32[128,4]{0,1:T(4,128)S(1)} %copy-done.3), channel_id=1, replica_groups=mesh['dp'=8,'label'=32] {'label'}, dimensions={0}, use_global_device_ids=true | all-gather | bytes 67584 | tf_op jit(solution)/shard_map/all_gather | solution.py:19
  175.7 5.1 %compare_reduce_fusion = pred[4096,512]{1,0:T(8,128)(4,1)S(1)} fusion(s32[512]{0:T(512)S(1)} %iota_add_fusion, s32[4096,4]{0,1:T(4,128)S(1)} %all_gather.7), kind=kLoop, calls=%fused_computation.4 | loop fusion | flops 14680064 | bytes 2164736 | tf_op jit(solution)/shard_map/reduce_or | solution.py:23
  180.9 9.2 %subtract_convert_fusion = bf16[4096,512]{1,0:T(8,128)(2,1)S(1)} fusion(pred[4096,512]{1,0:T(8,128)(4,1)S(1)} %compare_reduce_fusion, bf16[4096,1024]{1,0:T(8,128)(2,1)} %all-gather.2.cloned.1.call-done, bf16[512,1024]{1,0:T(8,128)(2,1)S(1)} %copy-done), kind=kOutput, calls=%fused_computation.7 | convolution fusion | flops 4307550208 | bytes 15728640 | tf_op jit(solution)/shard_map/dot_general | solution.py:20
  190.1 1.9 copy-done.5
  192.0 4.5 multiply_convert_fusion
  198.1 9.0 %convolution_convert_fusion = bf16[4096,1024]{1,0:T(8,128)(2,1)} fusion(bf16[4096,512]{1,0:T(8,128)(2,1)} %copy-done.5, bf16[512,1024]{1,0:T(8,128)(2,1)S(1)} %copy-done), kind=kOutput, calls=%fused_computation.8 | convolution fusion | flops 4299161600 | bytes 13631488 | tf_op jit(solution)/shard_map/dot_general | solution.py:30
  207.2 2.9 fusion.5
  210.1 2.5 copy.43
  212.6 5.5 %all-to-all-start.2 = ((bf16[32,32,1024]{2,1,0:T(8,128)(2,1)}), bf16[32,32,1024]{2,1,0:T(8,128)(2,1)S(1)}, u32[]{:S(2)}, u32[]{:S(2)}) async-start(bf16[32,32,1024]{2,1,0:T(8,128)(2,1)} %copy.43), calls=%async_computation.3 | async-start | bytes 4194304 | tf_op jit(solution)/shard_map/all_to_all | solution.py:72
  218.2 39.4 %all-to-all-done.2 = bf16[32,32,1024]{2,1,0:T(8,128)(2,1)S(1)} async-done(((bf16[32,32,1024]{2,1,0:T(8,128)(2,1)}), bf16[32,32,1024]{2,1,0:T(8,128)(2,1)S(1)}, u32[]{:S(2)}, u32[]{:S(2)}) %all-to-all-start.2) | async-done | bytes 2097184 | tf_op jit(solution)/shard_map/all_to_all | solution.py:72
  257.5 2.8 gather_fusion.2
  262.0 2.2 reduce_sum.19
  268.4 194.2 %reduce-scatter.8.cloned.1.call-done = bf16[128,1024]{1,0:T(8,128)(2,1)} async-done(((bf16[4096,1024]{1,0:T(8,128)(2,1)}), bf16[128,1024]{1,0:T(8,128)(2,1)}) %reduce-scatter.8.cloned.1.call-update) | async-done | bytes 262160 | tf_op jit(solution)/shard_map/reduce_scatter | solution.py:31
  462.7 1.9 add_convert_fusion
  (49 shorter events, 17.0 us)
Async XLA Ops:
  8.0 172.9 %copy-start = (bf16[512,1024]{1,0:T(8,128)(2,1)S(1)}, bf16[512,1024]{1,0:T(8,128)(2,1)}, u32[]{:S(2)}) copy-start(bf16[512,1024]{1,0:T(8,128)(2,1)} %param.8) | copy-start | bytes 3145732
  8.0 25.5 %copy-start.1 = (bf16[128,1024]{1,0:T(8,128)(2,1)S(1)}, bf16[128,1024]{1,0:T(8,128)(2,1)}, u32[]{:S(2)}) copy-start(bf16[128,1024]{1,0:T(8,128)(2,1)} %param.6) | copy-start | bytes 786436
  8.0 172.8 %all-gather.2.cloned.1.call-start = ((), (), s32[]{:S(2)}) async-start(), calls=%async_computation.6 | async-start | bytes 8650752 | tf_op jit(solution)/shard_map/all_gather | solution.py:18
  22.1 21.1 %all-to-all-start = ((s32[32,1,32]{2,1,0:T(1,128)}), s32[32,1,32]{2,1,0:T(1,128)S(1)}, u32[]{:S(2)}, u32[]{:S(2)}) async-start(s32[32,1,32]{2,1,0:T(1,128)} %bitcast.2), calls=%async_computation.1 | async-start | bytes 32768 | tf_op jit(solution)/shard_map/all_to_all | solution.py:59
  43.2 69.8 %all-to-all-start.1 = ((bf16[32,32,1024]{2,1,0:T(8,128)(2,1)}), bf16[32,32,1024]{2,1,0:T(8,128)(2,1)S(1)}, u32[]{:S(2)}, u32[]{:S(2)}) async-start(bf16[32,32,1024]{2,1,0:T(8,128)(2,1)} %broadcast_select_fusion), calls=%async_computation.2 | async-start | bytes 4194304 | tf_op jit(solution)/shard_map/all_to_all | solution.py:58
  48.9 215.3 %reduce-scatter.12.cloned.1.call-start = ((), (), s32[]{:S(2)}) async-start(), calls=%async_computation.9 | async-start | bytes 4718592
  113.0 2.3 copy-start.2
  126.8 0.7 copy-start.3
  126.9 139.8 %reduce-scatter.10.cloned.1.call-start = ((), (), s32[]{:S(2)}) async-start(), calls=%async_computation.8 | async-start | bytes 1179648
  180.9 11.1 %copy-start.4 = (bf16[4096,1024]{1,0:T(8,128)(2,1)S(1)}, bf16[4096,1024]{1,0:T(8,128)(2,1)}, u32[]{:S(2)}) copy-start(bf16[4096,1024]{1,0:T(8,128)(2,1)} %all-gather.2.cloned.1.call-done) | copy-start | bytes 25165828
  190.1 1.9 copy-start.5
  197.9 264.8 %reduce-scatter.8.cloned.1.call-start = ((), (), s32[]{:S(2)}) async-start(), calls=%async_computation.7 | async-start | bytes 8650752 | tf_op jit(solution)/shard_map/reduce_scatter | solution.py:31
  212.6 44.9 %all-to-all-start.2 = ((bf16[32,32,1024]{2,1,0:T(8,128)(2,1)}), bf16[32,32,1024]{2,1,0:T(8,128)(2,1)S(1)}, u32[]{:S(2)}, u32[]{:S(2)}) async-start(bf16[32,32,1024]{2,1,0:T(8,128)(2,1)} %copy.43), calls=%async_computation.3 | async-start | bytes 4194304 | tf_op jit(solution)/shard_map/all_to_all | solution.py:72
Sparse Core Ops, SparseCore 0:
  11.4 126.3 all-gather.1
Sparse Core Ops, SparseCore 1:
  126.9 34.5 reduce-scatter.11
  198.0 28.3 reduce-scatter.9
  230.2 232.4 reduce-scatter.7
where the time goes:
time: 473 us; the launch traced here: 472 us
  waiting for transfers between devices  302 us (64%)
  blocking collectives  48.2 us (10%)
  local copies, waits for them, and re-layouts  38.2 us (8%)
  matrix products  31.1 us (7%)
  starting transfers between devices  23 us (5%)
  between operations  15.9 us (3%)
  other arithmetic  13.4 us (3%)
    reduce_scatter x1, waiting for transfers between devices, per_device(): lax.psum_scatter(products.astype(jnp.bfloat16), 'label', scatter_dimensio...  194 us
    all_to_all x1, waiting for transfers between devices, per_device(): lax.all_to_all(send_rows, 'label', split_axis=0, concat_axis=0, tiled=True)  64 us
    all_gather x1, blocking collectives, per_device(): positives = lax.all_gather(positive_clusters, 'label', axis=0, tiled=True)  48.2 us
    all_to_all x1, waiting for transfers between devices, per_device(): lax.all_to_all(back.reshape(label_count, blocks_dev * capacity, width), '...  39.4 us
    unnamed x18, local copies, waits for them, and re-layouts  15.4 us
    all_to_all x1, starting transfers between devices, per_device(): lax.all_to_all(send_offsets, 'label', split_axis=0, concat_axis=0, tiled=...  11.3 us
  transfers between devices with their start and end apart: 7, of which 4 were waited for; matrix products, arithmetic and copies ran while one was open for 16% of the time, Pallas kernels for 0%

commit v1 on v0

--- a/solution.py
+++ b/solution.py
@@ -3,6 +3,28 @@
 import jax.numpy as jnp
 from jax import lax
 from jax.sharding import PartitionSpec as P
+
+
+def in_order(parts, dim):
+    lengths = list(parts.shape[1:])
+    lengths[dim] *= parts.shape[0]
+    return jnp.moveaxis(parts, 0, dim).reshape(lengths)
+
+
+def collected_by_bits(value, axis):
+    length = lax.axis_size(axis)
+    parts = value[None]
+    for level in range(length.bit_length() - 1):
+        bit = 1 << level
+        theirs = lax.ppermute(parts, axis, [(i, i ^ bit) for i in range(length)])
+        both = jnp.stack([parts, theirs])
+        upper = lax.axis_index(axis) >> level & 1
+        parts = jnp.where(upper == 0, both, both[::-1]).reshape(-1, *value.shape)
+    return parts
+
+
+def doubled_up(x, axis, dim):
+    return in_order(collected_by_bits(x, axis), dim)
 
 
 def per_device(
@@ -16,7 +38,7 @@
     scale = 1.0 / math.sqrt(rows_all * lax.axis_size("dp"))
     cluster_ids = label_index * clusters_dev + jnp.arange(clusters_dev, dtype=jnp.int32)
     rows = lax.all_gather(encoded, "label", axis=0, tiled=True)
-    positives = lax.all_gather(positive_clusters, "label", axis=0, tiled=True)
+    positives = doubled_up(positive_clusters, "label", 0)
     scores = lax.dot_general(
         rows, cluster_weight, (((1,), (1,)), ((), ())), preferred_element_type=jnp.float32
     )

time: 473 us -> 454 us (0.960)
  blocking collectives: 48.2 us -> 0 us
  waiting for transfers between devices: 302 us -> 320 us
  starting transfers between devices: 23 us -> 35 us
    all_gather x1 -> x0, blocking collectives: 48.2 us -> none  [per_device(): positives = lax.all_gather(positive_clusters, 'label', axis=0, tiled=True)]
    ppermute x0 -> x5, waiting for transfers between devices: none -> 13.9 us  [collected_by_bits(): theirs = lax.ppermute(parts, axis, [(i, i ^ bit) for i in range(length)])]
    ppermute x0 -> x5, starting transfers between devices: none -> 11.4 us  [collected_by_bits(): theirs = lax.ppermute(parts, axis, [(i, i ^ bit) for i in range(length)])]
    all_to_all x1, waiting for transfers between devices: 39.4 us -> 50 us  [per_device(): lax.all_to_all(back.reshape(label_count, blocks_dev * capacity, width), '...]
    reduce_scatter x1, waiting for transfers between devices: 194 us -> 187 us  [per_device(): lax.psum_scatter(products.astype(jnp.bfloat16), 'label', scatter_dimensio...]
    unnamed x18 -> x19, local copies, waits for them, and re-layouts: 15.4 us -> 15.5 us
  transfers between devices with their start and end apart: 7 -> 12, of which waited for: 4 -> 9; matrix products, arithmetic and copies ran while one was open for 16% -> 17% of each run, Pallas kernels for 0% -> 0%
where the time goes in v1:
time: 454 us; the launch traced here: 453 us
  waiting for transfers between devices  320 us (70%)
  local copies, waits for them, and re-layouts  38.3 us (8%)
  starting transfers between devices  35 us (8%)
  matrix products  31.2 us (7%)
  between operations  15.9 us (4%)
  other arithmetic  13.4 us (3%)
    reduce_scatter x1, waiting for transfers between devices, per_device(): lax.psum_scatter(products.astype(jnp.bfloat16), 'label', scatter_dimensio...  187 us
    all_to_all x1, waiting for transfers between devices, per_device(): lax.all_to_all(send_rows, 'label', split_axis=0, concat_axis=0, tiled=True)  64 us
    all_to_all x1, waiting for transfers between devices, per_device(): lax.all_to_all(back.reshape(label_count, blocks_dev * capacity, width), '...  50 us
    unnamed x19, local copies, waits for them, and re-layouts  15.5 us
    ppermute x5, waiting for transfers between devices, collected_by_bits(): theirs = lax.ppermute(parts, axis, [(i, i ^ bit) for i in range(length)])  13.9 us
    ppermute x5, starting transfers between devices, collected_by_bits(): theirs = lax.ppermute(parts, axis, [(i, i ^ bit) for i in range(length)])  11.4 us
    all_to_all x1, starting transfers between devices, per_device(): lax.all_to_all(send_offsets, 'label', split_axis=0, concat_axis=0, tiled=...  11.3 us
    dot_general x1, matrix products, per_device(): lax.dot_general(rows, cluster_weight, (((1,), (1,)), ((), ())), preferred...  9.33 us
  transfers between devices with their start and end apart: 12, of which 9 were waited for; matrix products, arithmetic and copies ran while one was open for 17% of the time, Pallas kernels for 0%

profile of v1, /device:TPU:8, one launch (start us, length us, event | category | flops | bytes accessed | tf_op | source)
XLA Modules:
  0.0 453.5 jit_solution(13284545659838967802)
XLA Ops:
  14.5 6.9 %gather_fusion = s32[1024]{0:T(1024)S(1)} fusion(s32[512]{0:T(512)S(1)} %reshape.108, s32[1024]{0:T(1024)S(1)} %maximum_clamp_fusion), kind=kCustom, calls=%fused_computation | custom fusion | bytes 12288 | tf_op jit(solution)/shard_map/gather | solution.py:76
  22.1 11.3 %all-to-all-start = ((s32[32,1,32]{2,1,0:T(1,128)}), s32[32,1,32]{2,1,0:T(1,128)S(1)}, u32[]{:S(2)}, u32[]{:S(2)}) async-start(s32[32,1,32]{2,1,0:T(1,128)} %bitcast.17), calls=%async_computation.1 | async-start | bytes 32768 | tf_op jit(solution)/shard_map/all_to_all | solution.py:81
  33.5 4.1 gather_fusion.1
  39.1 4.1 all-to-all-done
  43.2 5.7 %all-to-all-start.1 = ((bf16[32,32,1024]{2,1,0:T(8,128)(2,1)}), bf16[32,32,1024]{2,1,0:T(8,128)(2,1)S(1)}, u32[]{:S(2)}, u32[]{:S(2)}) async-start(bf16[32,32,1024]{2,1,0:T(8,128)(2,1)} %broadcast_select_fusion), calls=%async_computation.2 | async-start | bytes 4194304 | tf_op jit(solution)/shard_map/all_to_all | solution.py:80
  49.1 64.0 %all-to-all-done.1 = bf16[32,32,1024]{2,1,0:T(8,128)(2,1)S(1)} async-done(((bf16[32,32,1024]{2,1,0:T(8,128)(2,1)}), bf16[32,32,1024]{2,1,0:T(8,128)(2,1)S(1)}, u32[]{:S(2)}, u32[]{:S(2)}) %all-to-all-start.1) | async-done | bytes 2097184 | tf_op jit(solution)/shard_map/all_to_all | solution.py:80
  117.1 3.2 fusion
  120.3 6.5 %copy.55 = bf16[2048,1024]{0,1:T(8,128)(2,1)} copy(bf16[2048,1024]{1,0:T(8,128)(2,1)} %bitcast.94) | data formatting | bytes 8388608
  131.2 2.4 collective-permute-start.1
  135.8 3.3 collective-permute-start.2
  139.1 4.3 collective-permute-done.2
  144.5 2.7 collective-permute-done.3
  147.3 2.9 collective-permute-start.4
  150.2 2.8 collective-permute-done.4
  153.0 5.1 %compare_reduce_fusion = pred[4096,512]{1,0:T(8,128)(4,1)S(1)} fusion(s32[512]{0:T(512)S(1)} %iota_add_fusion, s32[4096,4]{0,1:T(4,128)S(1)} %bitcast.102), kind=kLoop, calls=%fused_computation.4 | loop fusion | flops 14680064 | bytes 2164736 | tf_op jit(solution)/shard_map/reduce_or | solution.py:45
  158.2 9.3 %subtract_convert_fusion = bf16[4096,512]{1,0:T(8,128)(2,1)S(1)} fusion(pred[4096,512]{1,0:T(8,128)(4,1)S(1)} %compare_reduce_fusion, bf16[4096,1024]{1,0:T(8,128)(2,1)} %all-gather.2.cloned.1.call-done, bf16[512,1024]{1,0:T(8,128)(2,1)S(1)} %copy-done), kind=kOutput, calls=%fused_computation.7 | convolution fusion | flops 4307550208 | bytes 15728640 | tf_op jit(solution)/shard_map/dot_general | solution.py:42
  169.5 4.5 multiply_convert_fusion
  175.6 9.0 %convolution_convert_fusion = bf16[4096,1024]{1,0:T(8,128)(2,1)} fusion(bf16[4096,512]{1,0:T(8,128)(2,1)} %copy-done.5, bf16[512,1024]{1,0:T(8,128)(2,1)S(1)} %copy-done), kind=kOutput, calls=%fused_computation.8 | convolution fusion | flops 4299161600 | bytes 13631488 | tf_op jit(solution)/shard_map/dot_general | solution.py:52
  184.6 2.9 fusion.5
  187.6 2.5 copy.50
  190.0 6.1 %all-to-all-start.2 = ((bf16[32,32,1024]{2,1,0:T(8,128)(2,1)}), bf16[32,32,1024]{2,1,0:T(8,128)(2,1)S(1)}, u32[]{:S(2)}, u32[]{:S(2)}) async-start(bf16[32,32,1024]{2,1,0:T(8,128)(2,1)} %copy.50), calls=%async_computation.3 | async-start | bytes 4194304 | tf_op jit(solution)/shard_map/all_to_all | solution.py:94
  196.2 50.0 %all-to-all-done.2 = bf16[32,32,1024]{2,1,0:T(8,128)(2,1)S(1)} async-done(((bf16[32,32,1024]{2,1,0:T(8,128)(2,1)}), bf16[32,32,1024]{2,1,0:T(8,128)(2,1)S(1)}, u32[]{:S(2)}, u32[]{:S(2)}) %all-to-all-start.2) | async-done | bytes 2097184 | tf_op jit(solution)/shard_map/all_to_all | solution.py:94
  246.2 2.8 gather_fusion.2
  257.1 186.9 %reduce-scatter.8.cloned.1.call-done = bf16[128,1024]{1,0:T(8,128)(2,1)} async-done(((bf16[4096,1024]{1,0:T(8,128)(2,1)}), bf16[128,1024]{1,0:T(8,128)(2,1)}) %reduce-scatter.8.cloned.1.call-update) | async-done | bytes 262160 | tf_op jit(solution)/shard_map/reduce_scatter | solution.py:53
  (71 shorter events, 34.1 us)
Async XLA Ops:
  8.0 150.2 %copy-start = (bf16[512,1024]{1,0:T(8,128)(2,1)S(1)}, bf16[512,1024]{1,0:T(8,128)(2,1)}, u32[]{:S(2)}) copy-start(bf16[512,1024]{1,0:T(8,128)(2,1)} %param.8) | copy-start | bytes 3145732
  8.0 25.5 %copy-start.1 = (bf16[128,1024]{1,0:T(8,128)(2,1)S(1)}, bf16[128,1024]{1,0:T(8,128)(2,1)}, u32[]{:S(2)}) copy-start(bf16[128,1024]{1,0:T(8,128)(2,1)} %param.6) | copy-start | bytes 786436
  8.0 150.2 %all-gather.2.cloned.1.call-start = ((), (), s32[]{:S(2)}) async-start(), calls=%async_computation.6 | async-start | bytes 8650752 | tf_op jit(solution)/shard_map/all_gather | solution.py:40
  22.1 21.1 %all-to-all-start = ((s32[32,1,32]{2,1,0:T(1,128)}), s32[32,1,32]{2,1,0:T(1,128)S(1)}, u32[]{:S(2)}, u32[]{:S(2)}) async-start(s32[32,1,32]{2,1,0:T(1,128)} %bitcast.17), calls=%async_computation.1 | async-start | bytes 32768 | tf_op jit(solution)/shard_map/all_to_all | solution.py:81
  43.2 69.9 %all-to-all-start.1 = ((bf16[32,32,1024]{2,1,0:T(8,128)(2,1)}), bf16[32,32,1024]{2,1,0:T(8,128)(2,1)S(1)}, u32[]{:S(2)}, u32[]{:S(2)}) async-start(bf16[32,32,1024]{2,1,0:T(8,128)(2,1)} %broadcast_select_fusion), calls=%async_computation.2 | async-start | bytes 4194304 | tf_op jit(solution)/shard_map/all_to_all | solution.py:80
  48.9 204.0 %reduce-scatter.12.cloned.1.call-start = ((), (), s32[]{:S(2)}) async-start(), calls=%async_computation.9 | async-start | bytes 4718592
  113.1 2.3 copy-start.2
  126.9 0.7 copy-start.3
  126.9 128.4 %reduce-scatter.10.cloned.1.call-start = ((), (), s32[]{:S(2)}) async-start(), calls=%async_computation.8 | async-start | bytes 1179648
  127.5 3.6 collective-permute-start
  131.2 4.6 %collective-permute-start.1 = (s32[2,128,4]{1,2,0:T(4,128)S(1)}, s32[2,128,4]{1,2,0:T(4,128)S(1)}, u32[]{:S(2)}, u32[]{:S(2)}) collective-permute-start(s32[2,128,4]{1,2,0:T(4,128)S(1)} %get-tuple-element.8), channel_id=1, source_target_pairs={{0,2},{1,3},{2,0},{3,1},{4,6},{5,7},{6,4},{7,5},{8,10},{9,11},{10,... | collective-permute-start | bytes 12296 | tf_op jit(solution)/shard_map/ppermute | solution.py:19
  135.8 7.6 %collective-permute-start.2 = (s32[4,128,4]{1,2,0:T(4,128)S(1)}, s32[4,128,4]{1,2,0:T(4,128)S(1)}, u32[]{:S(2)}, u32[]{:S(2)}) collective-permute-start(s32[4,128,4]{1,2,0:T(4,128)S(1)} %bitcast.109), channel_id=1, source_target_pairs={{0,4},{1,5},{2,6},{3,7},{4,0},{5,1},{6,2},{7,3},{8,12},{9,13},{10,... | collective-permute-start | bytes 24584 | tf_op jit(solution)/shard_map/ppermute | solution.py:19
  143.4 3.8 collective-permute-start.3
  147.3 5.7 %collective-permute-start.4 = (s32[16,128,4]{1,0,2:T(8,128)S(1)}, s32[16,128,4]{1,0,2:T(8,128)S(1)}, u32[]{:S(2)}, u32[]{:S(2)}) collective-permute-start(s32[16,128,4]{1,0,2:T(8,128)S(1)} %get-tuple-element.6), channel_id=1, source_target_pairs={{0,16},{1,17},{2,18},{3,19},{4,20},{5,21},{6,22},{7,23},{8,24},{9,... | collective-permute-start | bytes 98312 | tf_op jit(solution)/shard_map/ppermute | solution.py:19
  158.2 11.3 %copy-start.4 = (bf16[4096,1024]{1,0:T(8,128)(2,1)S(1)}, bf16[4096,1024]{1,0:T(8,128)(2,1)}, u32[]{:S(2)}) copy-start(bf16[4096,1024]{1,0:T(8,128)(2,1)} %all-gather.2.cloned.1.call-done) | copy-start | bytes 25165828
  167.6 1.9 copy-start.5
  175.4 268.6 %reduce-scatter.8.cloned.1.call-start = ((), (), s32[]{:S(2)}) async-start(), calls=%async_computation.7 | async-start | bytes 8650752 | tf_op jit(solution)/shard_map/reduce_scatter | solution.py:53
  190.0 56.2 %all-to-all-start.2 = ((bf16[32,32,1024]{2,1,0:T(8,128)(2,1)}), bf16[32,32,1024]{2,1,0:T(8,128)(2,1)S(1)}, u32[]{:S(2)}, u32[]{:S(2)}) async-start(bf16[32,32,1024]{2,1,0:T(8,128)(2,1)} %copy.50), calls=%async_computation.3 | async-start | bytes 4194304 | tf_op jit(solution)/shard_map/all_to_all | solution.py:94
Sparse Core Ops, SparseCore 0:
  11.4 126.2 all-gather.1
Sparse Core Ops, SparseCore 1:
  127.0 34.5 reduce-scatter.11
  175.5 28.8 reduce-scatter.9
  208.2 235.7 reduce-scatter.7
